TPU v7x, 32 devices: a whole 2x2x4 slice. The times are simulated.
32 devices in a mesh: snap: 4 (over x, core), slab: 8 (over z, y).
Axes of the slice: x: 2, y: 2, z: 4, core: 2. Of those that a mesh axis runs over, the one named last changes fastest.
Arguments:
- velocity: bfloat16 [256, 3, 40, 8, 128], P('snap', None, 'slab'), may hold values from -10 to 10
Outputs:
- modes: bfloat16 [768, 8, 5120], P(None, 'slab', 'snap')
- factor: float32 [768, 768], replicated
All inputs are finite; a program needn't handle non-finite values.
Results may differ from a plain program's by a relative error of at most 0.0004.
The roundings to bfloat16 on the way count: a program that leaves them out, or rounds other values in their place, can miss the bound.
Values may be sent and summed in bfloat16 or wider, within the bound.
A program may use at most 64 MiB of HBM per device.

v0:
```python
import jax
import jax.numpy as jnp
from jax import lax
from jax.sharding import PartitionSpec as P

stencil_weights = (4.0 / 5.0, -1.0 / 5.0, 4.0 / 105.0, -1.0 / 280.0)


def with_halo(block, sides, width):
    for axis, dim in sides:
        count = lax.axis_size(axis)
        forward = [(i, i + 1) for i in range(count - 1)]
        backward = [(target, source) for source, target in forward]
        low = lax.ppermute(
            lax.slice_in_dim(block, block.shape[dim] - width, None, axis=dim), axis, forward
        )
        high = lax.ppermute(lax.slice_in_dim(block, 0, width, axis=dim), axis, backward)
        block = jnp.concatenate([low, block, high], axis=dim)
    return block


def differ(padded, axis, length):
    total = None
    for offset in range(4):
        step = offset + 1
        ahead = lax.slice_in_dim(padded, 4 + step, 4 + step + length, axis=axis)
        behind = lax.slice_in_dim(padded, 4 - step, 4 - step + length, axis=axis)
        term = stencil_weights[offset] * (ahead - behind)
        total = term if total is None else total + term
    return total


def derive(field, axis):
    widths = [(0, 0)] * field.ndim
    widths[axis] = (4, 4)
    return differ(jnp.pad(field, widths), axis, field.shape[axis])


def reduce_entries(entries):
    share = lax.psum_scatter(entries, ("snap", "slab"), scatter_dimension=0, tiled=True)
    total = lax.all_gather(share, ("snap", "slab"), axis=0, tiled=True)
    return total


def padded_sum(entries):
    summed = reduce_entries(entries)
    return summed


def body(velocity):
    planes = velocity.shape[2]
    extended = with_halo(velocity[:, 1:3], (("slab", 2),), 4)
    second_rim = extended[:, 0].astype(jnp.float32)
    third_rim = extended[:, 1].astype(jnp.float32)
    first = velocity[:, 0].astype(jnp.float32)
    second = velocity[:, 1].astype(jnp.float32)
    third = velocity[:, 2].astype(jnp.float32)
    omega_one = derive(third, 2) - derive(second, 3)
    omega_two = derive(first, 3) - differ(third_rim, 1, planes)
    omega_three = differ(second_rim, 1, planes) - derive(first, 2)
    vorticity = jnp.stack([omega_one, omega_two, omega_three], axis=1).astype(jnp.bfloat16)
    local_snaps = vorticity.shape[0]
    flat = vorticity.reshape(local_snaps, 3, -1)
    regrouped = lax.all_to_all(flat, "snap", split_axis=2, concat_axis=0, tiled=True)
    width = regrouped.shape[0] * 3
    matrix = regrouped.reshape(width, -1)
    rows = matrix.shape[1]
    gram = lax.dot_general(
        matrix, matrix, (((1,), (1,)), ((), ())), preferred_element_type=jnp.float32
    )
    total = padded_sum(gram.reshape(-1)).reshape(width, width)
    point_count = rows * lax.axis_size("snap") * lax.axis_size("slab")
    lower = jnp.linalg.cholesky(total / point_count)
    factor = lower.T
    solved = jax.scipy.linalg.solve_triangular(lower, matrix.astype(jnp.float32), lower=True)
    modes = solved.astype(jnp.bfloat16).reshape(width, 1, rows)
    return (modes, factor)


def solution(mesh):
    in_specs = (P("snap", None, "slab", None, None),)
    out_specs = (P(None, "slab", "snap"), P())
    return jax.shard_map(body, mesh=mesh, in_specs=in_specs, out_specs=out_specs, check_vma=False)
```

profile of v0, /device:TPU:0, one launch (start us, length us, event | category | flops | bytes accessed | tf_op | source)
XLA Modules:
  0.0 584.6 jit_solution(12519022883686807485)
XLA Ops:
  7.2 3.2 fusion.116
  10.4 1.1 copy.52
  11.5 1.3 collective-permute-start.1
  12.8 6.5 %collective-permute-start = (bf16[64,2,4,8,128]{4,3,2,1,0:T(8,128)(2,1)}, bf16[64,2,4,8,128]{4,3,2,1,0:T(8,128)(2,1)}, u32[]{:S(2)}, u32[]{:S(2)}) collective-permute-start(bf16[64,2,4,8,128]{4,3,2,1,0:T(8,128)(2,1)} %get-tuple-element.38), channel_id=1, source_target_pairs={{0,1},{1,2},{2,3},{3,4},{4,5},{5,6},{6,7},{8,9},{9,10},{10,11},{11... | collective-permute-start | bytes 3145736 | tf_op jit(solution)/shard_map/ppermute | solution.py:14
  20.3 3.3 fusion.66
  23.7 2.1 stack.12
  25.8 36.6 %collective-permute-done = bf16[64,2,4,8,128]{4,3,2,1,0:T(8,128)(2,1)} collective-permute-done((bf16[64,2,4,8,128]{4,3,2,1,0:T(8,128)(2,1)}, bf16[64,2,4,8,128]{4,3,2,1,0:T(8,128)(2,1)}, u32[]{:S(2)}, u32[]{:S(2)}) %collective-permute-start) | collective-permute-done | bytes 1048608 | tf_op jit(solution)/shard_map/ppermute | solution.py:14
  62.4 1.3 copy_dynamic-update-slice_fusion.1
  64.0 1.4 constant_dynamic-update-slice_fusion
  65.8 4.7 fusion.29
  70.8 1.1 stack.14
  71.9 1.3 pad_maximum_fusion
  73.2 5.1 copy.42
  78.3 5.3 reshape.205
  83.7 27.5 %all_to_all.15 = bf16[4,2,122880]{2,1,0:T(2,128)(2,1)} all-to-all(bf16[4,2,122880]{2,1,0:T(2,128)(2,1)S(1)} %reshape.205), channel_id=1, replica_groups=mesh['snap'=4,'slab'=8] {'snap'}, dimensions={0} | all-to-all | bytes 3932160 | tf_op jit(solution)/shard_map/all_to_all | solution.py:64
  111.2 6.2 %reshape.206 = bf16[5120,3,64]{2,1,0:T(4,128)(2,1)} reshape(bf16[4,2,122880]{2,1,0:T(2,128)(2,1)} %all_to_all.15) | data formatting | bytes 3932160
  117.4 7.8 %copy.44 = bf16[4,64,3,1280]{3,2,1,0:T(4,128)(2,1)S(1)} copy(bf16[4,64,3,1280]{1,2,3,0:T(4,128)(2,1)} %bitcast.129) | data formatting | bytes 3932160 | tf_op jit(solution)/shard_map/all_to_all | solution.py:64
  125.2 2.8 reshape.179
  128.0 3.9 fusion.117
  131.9 1.6 reshape.180
  133.5 135.5 %all-reduce.8.cloned.1.call-done = f32[589824]{0:T(1024)} async-done(((f32[589824]{0:T(1024)}), f32[589824]{0:T(1024)}) %all-reduce.8.cloned.1.call-update) | async-done | bytes 2359312
  269.0 1.5 dynamic-slice.3
  270.6 2.2 convert_element_type.53
  272.7 56.5 %all-gather.2.cloned.1.call-done = f32[589824]{0:T(1024)} async-done(((f32[18432]{0:T(1024)}), f32[589824]{0:T(1024)}) %all-gather.2.cloned.1.call-update) | async-done | bytes 2359312 | tf_op jit(solution)/shard_map/all_gather | solution.py:41
  329.2 3.3 broadcast_multiply_fusion
  332.5 2.5 div.18
  335.0 2.1 copy.45
  337.1 2.0 fusion.11
  339.1 1.4 copy-done.3
  340.5 11.7 %cholesky.165 = f32[128,128]{1,0:T(8,128)S(1)} custom-call(f32[128,128]{1,0:T(8,128)S(1)} %cholesky.424), custom_call_target="Cholesky" | custom-call | tf_op jit(solution)/shard_map/jit(cholesky)/cholesky | solution.py:73
  352.2 9.8 %custom-call.47 = f32[1,128,128]{1,2,0:T(8,128)S(1)} custom-call(f32[1,128,128]{2,1,0:T(8,128)S(1)} %get-tuple-element.56), custom_call_target="InvertDiagBlocksLowerTriangular" | custom-call | tf_op jit(solution)/shard_map/jit(cholesky)/cholesky | solution.py:73
  362.2 1.4 constant_dynamic-update-slice_fusion.11
  363.6 1.4 convolution_subtract_fusion.4
  365.0 11.7 %cholesky.188 = f32[128,128]{1,0:T(8,128)S(1)} custom-call(f32[128,128]{1,0:T(8,128)S(1)} %cholesky.428), custom_call_target="Cholesky" | custom-call | tf_op jit(solution)/shard_map/jit(cholesky)/cholesky | solution.py:73
  376.8 10.0 %custom-call.48 = f32[1,128,128]{1,2,0:T(8,128)S(1)} custom-call(f32[1,128,128]{2,1,0:T(8,128)S(1)} %get-tuple-element.53), custom_call_target="InvertDiagBlocksLowerTriangular" | custom-call | tf_op jit(solution)/shard_map/jit(cholesky)/cholesky | solution.py:73
  387.1 1.5 convolution_subtract_fusion.5
  388.7 11.7 %cholesky.354 = f32[128,128]{1,0:T(8,128)S(1)} custom-call(f32[128,128]{1,0:T(8,128)S(1)} %cholesky.433), custom_call_target="Cholesky" | custom-call | tf_op jit(solution)/shard_map/jit(cholesky)/cholesky | solution.py:73
  401.1 9.8 %custom-call.49 = f32[1,128,128]{1,2,0:T(8,128)S(1)} custom-call(f32[1,128,128]{2,1,0:T(8,128)S(1)} %get-tuple-element.50), custom_call_target="InvertDiagBlocksLowerTriangular" | custom-call | tf_op jit(solution)/shard_map/jit(cholesky)/cholesky | solution.py:73
  411.2 1.6 convolution_subtract_fusion.6
  412.8 12.2 %cholesky.373 = f32[128,128]{1,0:T(8,128)S(1)} custom-call(f32[128,128]{1,0:T(8,128)S(1)} %cholesky.438), custom_call_target="Cholesky" | custom-call | tf_op jit(solution)/shard_map/jit(cholesky)/cholesky | solution.py:73
  425.7 9.8 %custom-call.50 = f32[1,128,128]{1,2,0:T(8,128)S(1)} custom-call(f32[1,128,128]{2,1,0:T(8,128)S(1)} %get-tuple-element.47), custom_call_target="InvertDiagBlocksLowerTriangular" | custom-call | tf_op jit(solution)/shard_map/jit(cholesky)/cholesky | solution.py:73
  435.8 1.5 convolution_subtract_fusion.7
  437.3 11.7 %cholesky.392 = f32[128,128]{1,0:T(8,128)S(1)} custom-call(f32[128,128]{1,0:T(8,128)S(1)} %cholesky.443), custom_call_target="Cholesky" | custom-call | tf_op jit(solution)/shard_map/jit(cholesky)/cholesky | solution.py:73
  449.7 9.8 %custom-call.51 = f32[1,128,128]{1,2,0:T(8,128)S(1)} custom-call(f32[1,128,128]{2,1,0:T(8,128)S(1)} %get-tuple-element.44), custom_call_target="InvertDiagBlocksLowerTriangular" | custom-call | tf_op jit(solution)/shard_map/jit(cholesky)/cholesky | solution.py:73
  459.7 1.3 convolution_subtract_fusion.8
  461.0 11.9 %cholesky.410 = f32[128,128]{1,0:T(8,128)S(1)} custom-call(f32[128,128]{1,0:T(8,128)S(1)} %convolution_subtract_fusion.8), custom_call_target="Cholesky" | custom-call | tf_op jit(solution)/shard_map/jit(cholesky)/cholesky | solution.py:73
  477.9 2.5 fusion.20
  480.4 3.0 copy.46
  483.5 17.0 %while.1 = (s32[]{:T(128)}, f32[768,768]{1,0:T(8,128)}, s32[6,2]{0,1:T(2,128)S(1)}, f32[6,128,128]{2,1,0:T(8,128)S(1)}, s32[]{:T(128)}) while((s32[]{:T(128)}, f32[768,768]{1,0:T(8,128)}, s32[6,2]{0,1:T(2,128)S(1)}, f32[6,128,128]{2,1,0:T(8,128)S(1)}, s32[]{:T(128)}) %tuple.51), condition=%wide.while_cond, body=%wide.while_body.sunk | while | flops 2 | bytes 131189 | solution.py:75
  484.1 2.2 bitcast_dynamic-update-slice_fusion.7
  486.9 2.2 bitcast_dynamic-update-slice_fusion.7
  489.8 2.2 bitcast_dynamic-update-slice_fusion.7
  492.6 2.2 bitcast_dynamic-update-slice_fusion.7
  495.5 2.2 bitcast_dynamic-update-slice_fusion.7
  498.3 2.1 bitcast_dynamic-update-slice_fusion.7
  500.5 59.0 %custom-call.52 = f32[6,128,128]{1,2,0:T(8,128)S(1)} custom-call(f32[6,128,128]{2,1,0:T(8,128)S(1)} %get-tuple-element.9), custom_call_target="InvertDiagBlocksLowerTriangular" | custom-call | tf_op jit(solution)/shard_map/jit(_solve_triangular)/triangular_solve | solution.py:75
  559.4 1.4 bitcast_dynamic-update-slice_fusion.5
  560.9 1.9 convolution_subtract_fusion.3
  563.7 1.7 convolution_subtract_fusion.2
  566.1 2.2 convolution_subtract_fusion.1
  568.4 0.7 bitcast_dynamic-update-slice_fusion.2
  569.1 2.4 fusion.8
  572.6 3.0 convolution_subtract_fusion
  576.3 1.3 copy-done.5
  (66 shorter events, 13.8 us)
Async XLA Ops:
  7.2 261.8 %all-reduce.8.cloned.1.call-start = ((), (), s32[]{:S(2)}) async-start(), calls=%async_computation.2 | async-start | bytes 4718592
  10.4 8.9 %copy-start = (bf16[64,3,5,8,128]{4,3,2,1,0:T(8,128)(2,1)S(1)}, bf16[64,3,5,8,128]{4,3,2,1,0:T(8,128)(2,1)}, u32[]{:S(2)}) copy-start(bf16[64,3,5,8,128]{4,3,2,1,0:T(8,128)(2,1)} %param.1) | copy-start | bytes 5898244
  11.5 52.5 %collective-permute-start.1 = (bf16[64,2,4,8,128]{4,3,2,0,1:T(8,128)(2,1)}, bf16[64,2,4,8,128]{4,3,2,0,1:T(8,128)(2,1)}, u32[]{:S(2)}, u32[]{:S(2)}) collective-permute-start(bf16[64,2,4,8,128]{4,3,2,0,1:T(8,128)(2,1)} %copy.52), channel_id=1, source_target_pairs={{1,0},{2,1},{3,2},{4,3},{5,4},{6,5},{7,6},{9,8},{10,9},{11,10},{12... | collective-permute-start | bytes 3145736 | tf_op jit(solution)/shard_map/ppermute | solution.py:17
  12.8 49.7 %collective-permute-start = (bf16[64,2,4,8,128]{4,3,2,1,0:T(8,128)(2,1)}, bf16[64,2,4,8,128]{4,3,2,1,0:T(8,128)(2,1)}, u32[]{:S(2)}, u32[]{:S(2)}) collective-permute-start(bf16[64,2,4,8,128]{4,3,2,1,0:T(8,128)(2,1)} %get-tuple-element.38), channel_id=1, source_target_pairs={{0,1},{1,2},{2,3},{3,4},{4,5},{5,6},{6,7},{8,9},{9,10},{10,11},{11... | collective-permute-start | bytes 3145736 | tf_op jit(solution)/shard_map/ppermute | solution.py:14
  70.5 1.4 copy-start.4
  133.4 137.1 %copy-start.2 = (bf16[768,1280]{1,0:T(8,128)(2,1)S(1)}, bf16[768,1280]{1,0:T(8,128)(2,1)}, u32[]{:S(2)}) copy-start(bf16[768,1280]{1,0:T(8,128)(2,1)} %reshape.179) | copy-start | bytes 5898244
  133.4 195.8 %all-gather.2.cloned.1.call-start = ((), (), s32[]{:S(2)}) async-start(), calls=%async_computation.1 | async-start | bytes 2433024 | tf_op jit(solution)/shard_map/all_gather | solution.py:41
  339.0 1.4 copy-start.3
  560.9 2.8 copy-start.1
  576.3 1.3 copy-start.5
Sparse Core Ops, SparseCore 0:
  133.6 135.3 all-reduce.7
  272.9 56.2 all-gather.1
where the time goes:
time: 595 us; the launch traced here: 585 us
  waiting for transfers between devices  229 us (38%)
  other arithmetic  203 us (34%)
  local copies, waits for them, and re-layouts  68.6 us (12%)
  matrix products  30.2 us (5%)
  blocking collectives  27.5 us (5%)
  between operations  18.4 us (3%)
  starting transfers between devices  7.9 us (1%)
    unnamed x3, waiting for transfers between devices  136 us
    another operation x22, other arithmetic, body(): lower = jnp.linalg.cholesky(total / point_count)  124 us
    another operation x2, other arithmetic, body(): jax.scipy.linalg.solve_triangular(lower, matrix.astype(jnp.float32), lowe...  59 us
    all_gather x1, waiting for transfers between devices, reduce_entries(): total = lax.all_gather(share, ('snap', 'slab'), axis=0, tiled=True)  56.5 us
    ppermute x1, waiting for transfers between devices, with_halo(): lax.ppermute(lax.slice_in_dim(block, block.shape[dim] - width, None, axis...  36.6 us
    all_to_all x1, blocking collectives, body(): lax.all_to_all(flat, 'snap', split_axis=2, concat_axis=0, tiled=True)  27.5 us
    unnamed x23, local copies, waits for them, and re-layouts  21.5 us
    another operation x18, local copies, waits for them, and re-layouts  16.9 us
  transfers between devices with their start and end apart: 4, of which 3 were waited for; matrix products, arithmetic and copies ran while one was open for 2% of the time, Pallas kernels for 0%

commit v1 on v0

--- a/solution.py
+++ b/solution.py
@@ -1,9 +1,16 @@
+import functools
 import jax
 import jax.numpy as jnp
 from jax import lax
+from jax.experimental import pallas as pl
+from jax.experimental.pallas import tpu as pltpu
 from jax.sharding import PartitionSpec as P
 
 stencil_weights = (4.0 / 5.0, -1.0 / 5.0, 4.0 / 105.0, -1.0 / 280.0)
+MESH = pl.DeviceIdType.MESH
+HI = lax.Precision.HIGHEST
+BLOCK = 128
+VMEM_LIMIT = 48 * 1024 * 1024
 
 
 def with_halo(block, sides, width):
@@ -36,15 +43,246 @@
     return differ(jnp.pad(field, widths), axis, field.shape[axis])
 
 
-def reduce_entries(entries):
-    share = lax.psum_scatter(entries, ("snap", "slab"), scatter_dimension=0, tiled=True)
-    total = lax.all_gather(share, ("snap", "slab"), axis=0, tiled=True)
-    return total
-
-
-def padded_sum(entries):
-    summed = reduce_entries(entries)
-    return summed
+def upper_offsets(blocks):
+    starts, at = [], 0
+    for i in range(blocks):
+        starts.append(at)
+        at += (blocks - i) * BLOCK
+    return starts, at
+
+
+def halving_steps(snap, slab):
+    steps = []
+    for axis, count in (("snap", snap), ("slab", slab)):
+        bit = 1
+        while bit < count:
+            steps.append((axis, bit))
+            bit *= 2
+    return steps
+
+
+def gram_kernel(steps, m_ref, out_ref, acc_ref, landing, send_sem, recv_sem, gather_send, gather_recv):
+    width = m_ref.shape[0]
+    blocks = width // BLOCK
+    total_rows = acc_ref.shape[0]
+    place = {"snap": lax.axis_index("snap"), "slab": lax.axis_index("slab")}
+
+    def partner(axis, bit):
+        own = place[axis]
+        is_high = lax.rem(own // bit, 2)
+        return is_high, {**place, axis: own + bit - 2 * bit * is_high}
+
+    def device(where):
+        return (where["snap"], where["slab"])
+
+    barrier = pltpu.get_barrier_semaphore()
+    for axis, bit in steps:
+        pl.semaphore_signal(barrier, 1, device_id=device(partner(axis, bit)[1]), device_id_type=MESH)
+
+    starts, used = upper_offsets(blocks)
+    for i in range(blocks):
+        tall = lax.dot_general(
+            m_ref[i * BLOCK :, :],
+            m_ref[i * BLOCK : (i + 1) * BLOCK, :],
+            (((1,), (1,)), ((), ())),
+            preferred_element_type=jnp.float32,
+        )
+        acc_ref[starts[i] : starts[i] + (blocks - i) * BLOCK, :] = tall
+    if total_rows > used:
+        acc_ref[used:, :] = jnp.zeros((total_rows - used, BLOCK), jnp.float32)
+    pl.semaphore_wait(barrier, len(steps))
+
+    start, length, at = 0, total_rows, 0
+    history = []
+    for index, (axis, bit) in enumerate(steps):
+        half = length // 2
+        is_high, other = partner(axis, bit)
+        keep = pl.multiple_of(start + is_high * half, 8)
+        give = pl.multiple_of(start + (1 - is_high) * half, 8)
+        copy = pltpu.make_async_remote_copy(
+            src_ref=acc_ref.at[pl.ds(give, half)],
+            dst_ref=landing.at[pl.ds(at, half)],
+            send_sem=send_sem.at[index],
+            recv_sem=recv_sem.at[index],
+            device_id=device(other),
+            device_id_type=MESH,
+        )
+        copy.start()
+        copy.wait()
+        acc_ref[pl.ds(keep, half), :] = acc_ref[pl.ds(keep, half), :] + landing[at : at + half, :]
+        history.append((index, axis, bit, keep, half))
+        start, length, at = keep, half, at + half
+    out_ref[pl.ds(start, length), :] = acc_ref[pl.ds(start, length), :]
+    for index, axis, bit, keep, half in reversed(history):
+        other = partner(axis, bit)[1]
+        copy = pltpu.make_async_remote_copy(
+            src_ref=out_ref.at[pl.ds(keep, half)],
+            dst_ref=out_ref.at[pl.ds(keep, half)],
+            send_sem=gather_send.at[index],
+            recv_sem=gather_recv.at[index],
+            device_id=device(other),
+            device_id_type=MESH,
+        )
+        copy.start()
+        copy.wait()
+
+
+def summed_gram(matrix, snap, slab):
+    width, points = matrix.shape
+    used = upper_offsets(width // BLOCK)[1]
+    devices = snap * slab
+    share = -(-used // (devices * 8)) * 8
+    rows = share * devices
+    steps = halving_steps(snap, slab)
+    count = max(len(steps), 1)
+    return pl.pallas_call(
+        functools.partial(gram_kernel, steps),
+        out_shape=jax.ShapeDtypeStruct((rows, BLOCK), jnp.float32),
+        in_specs=[pl.BlockSpec(memory_space=pltpu.VMEM)],
+        out_specs=pl.BlockSpec(memory_space=pltpu.VMEM),
+        scratch_shapes=[
+            pltpu.VMEM((rows, BLOCK), jnp.float32),
+            pltpu.VMEM((rows, BLOCK), jnp.float32),
+            pltpu.SemaphoreType.DMA((count,)),
+            pltpu.SemaphoreType.DMA((count,)),
+            pltpu.SemaphoreType.DMA((count,)),
+            pltpu.SemaphoreType.DMA((count,)),
+        ],
+        compiler_params=pltpu.CompilerParams(
+            collective_id=1, has_side_effects=True, vmem_limit_bytes=VMEM_LIMIT
+        ),
+        name="gram_sum",
+    )(matrix)
+
+
+def factor_diagonal(d_ref, w_ref, out_ref, spread):
+    group = 8
+    count = BLOCK // group
+    for g in range(count):
+        lo = g * group
+        tile = d_ref[lo : lo + group, :]
+        for k in range(group):
+            spread[g % 2, k] = jnp.broadcast_to(tile[:, lo + k : lo + k + 1], (group, BLOCK))
+        a = [[spread[g % 2, k, i : i + 1, :] for k in range(i + 1)] for i in range(group)]
+        mult = [[None] * group for _ in range(group)]
+        inv = [None] * group
+        root = [None] * group
+        for k in range(group):
+            inv[k] = 1.0 / a[k][k]
+            root[k] = lax.rsqrt(a[k][k])
+            for i in range(k + 1, group):
+                mult[i][k] = a[i][k] * inv[k]
+            for i in range(k + 1, group):
+                for j in range(k + 1, i + 1):
+                    a[i][j] = a[i][j] - mult[i][k] * a[j][k]
+        rows = [d_ref[lo + i : lo + i + 1, :] for i in range(group)]
+        sides = [w_ref[lo + i : lo + i + 1, :] for i in range(group)]
+        for k in range(group):
+            for i in range(k + 1, group):
+                rows[i] = rows[i] - mult[i][k] * rows[k]
+                sides[i] = sides[i] - mult[i][k] * sides[k]
+        for i in range(group):
+            out_ref[lo + i : lo + i + 1, :] = sides[i] * root[i]
+        for t in range(g + 1, count):
+            below = d_ref[t * group : (t + 1) * group, :]
+            aside = w_ref[t * group : (t + 1) * group, :]
+            columns = [
+                jnp.broadcast_to(below[:, lo + k : lo + k + 1], (group, BLOCK)) for k in range(group)
+            ]
+            for k in range(group):
+                for i in range(k + 1, group):
+                    columns[i] = columns[i] - mult[i][k] * columns[k]
+            for k in range(group):
+                scaled = columns[k] * inv[k]
+                below = below - scaled * rows[k]
+                aside = aside - scaled * sides[k]
+            d_ref[t * group : (t + 1) * group, :] = below
+            w_ref[t * group : (t + 1) * group, :] = aside
+
+
+def solve_kernel(points, g_ref, m_ref, modes_ref, factor_ref, work, inverse, diag, side, dinv, spread):
+    width = m_ref.shape[0]
+    blocks = width // BLOCK
+    starts, _ = upper_offsets(blocks)
+    rank = lax.broadcasted_iota(jnp.int32, (BLOCK, BLOCK), 0)
+    lane = lax.broadcasted_iota(jnp.int32, (BLOCK, BLOCK), 1)
+    eye = jnp.where(rank == lane, 1.0, 0.0).astype(jnp.float32)
+    zero = jnp.zeros((BLOCK, BLOCK), jnp.float32)
+    for i in range(blocks):
+        for j in range(blocks):
+            here = (slice(i * BLOCK, (i + 1) * BLOCK), slice(j * BLOCK, (j + 1) * BLOCK))
+            there = (here[0], slice(width + j * BLOCK, width + (j + 1) * BLOCK))
+            if j >= i:
+                row = starts[i] + (j - i) * BLOCK
+                block = g_ref[row : row + BLOCK, :] / points
+                work[here] = block if i == j else block.T
+            else:
+                work[here] = zero
+            work[there] = eye if i == j else zero
+
+    def step(k, carry):
+        base = pl.multiple_of(k * BLOCK, BLOCK)
+        diag[...] = work[pl.ds(base, BLOCK), pl.ds(base, BLOCK)]
+        side[...] = eye
+        factor_diagonal(diag, side, dinv, spread)
+        panel = jnp.dot(
+            dinv[...], work[pl.ds(base, BLOCK), :], precision=HI, preferred_element_type=jnp.float32
+        )
+        work[pl.ds(base, BLOCK), :] = panel
+
+        def update(i, inner):
+            low = pl.multiple_of(i * BLOCK, BLOCK)
+            left = work[pl.ds(base, BLOCK), pl.ds(low, BLOCK)].T
+            work[pl.ds(low, BLOCK), :] -= jnp.dot(
+                left, work[pl.ds(base, BLOCK), :], precision=HI, preferred_element_type=jnp.float32
+            )
+            return inner
+
+        lax.fori_loop(k + 1, blocks, update, 0)
+        return carry
+
+    lax.fori_loop(0, blocks, step, 0)
+    for i in range(blocks):
+        rows = slice(i * BLOCK, (i + 1) * BLOCK)
+        for j in range(blocks):
+            cols = slice(j * BLOCK, (j + 1) * BLOCK)
+            if j < i:
+                factor_ref[rows, cols] = zero
+            elif j == i:
+                factor_ref[rows, cols] = jnp.where(lane >= rank, work[rows, cols], 0.0)
+            else:
+                factor_ref[rows, cols] = work[rows, cols]
+        depth = (i + 1) * BLOCK
+        part = work[rows, width : width + depth]
+        top = part.astype(jnp.bfloat16)
+        rest = (part - top.astype(jnp.float32)).astype(jnp.bfloat16)
+        solved = jnp.dot(top, m_ref[:depth, :], preferred_element_type=jnp.float32)
+        solved = solved + jnp.dot(rest, m_ref[:depth, :], preferred_element_type=jnp.float32)
+        modes_ref[rows, :] = solved.astype(jnp.bfloat16)
+
+
+def factor_and_solve(gram, matrix, points):
+    width, count = matrix.shape
+    vmem = pl.BlockSpec(memory_space=pltpu.VMEM)
+    return pl.pallas_call(
+        functools.partial(solve_kernel, float(points)),
+        out_shape=(
+            jax.ShapeDtypeStruct((width, count), jnp.bfloat16),
+            jax.ShapeDtypeStruct((width, width), jnp.float32),
+        ),
+        in_specs=[vmem, vmem],
+        out_specs=(vmem, vmem),
+        scratch_shapes=[
+            pltpu.VMEM((width, 2 * width), jnp.float32),
+            pltpu.VMEM((8, BLOCK), jnp.float32),
+            pltpu.VMEM((BLOCK, BLOCK), jnp.float32),
+            pltpu.VMEM((BLOCK, BLOCK), jnp.float32),
+            pltpu.VMEM((BLOCK, BLOCK), jnp.float32),
+            pltpu.VMEM((2, 8, 8, BLOCK), jnp.float32),
+        ],
+        compiler_params=pltpu.CompilerParams(vmem_limit_bytes=VMEM_LIMIT),
+        name="factor_solve",
+    )(gram, matrix)
 
 
 def body(velocity):
@@ -65,16 +303,10 @@
     width = regrouped.shape[0] * 3
     matrix = regrouped.reshape(width, -1)
     rows = matrix.shape[1]
-    gram = lax.dot_general(
-        matrix, matrix, (((1,), (1,)), ((), ())), preferred_element_type=jnp.float32
-    )
-    total = padded_sum(gram.reshape(-1)).reshape(width, width)
-    point_count = rows * lax.axis_size("snap") * lax.axis_size("slab")
-    lower = jnp.linalg.cholesky(total / point_count)
-    factor = lower.T
-    solved = jax.scipy.linalg.solve_triangular(lower, matrix.astype(jnp.float32), lower=True)
-    modes = solved.astype(jnp.bfloat16).reshape(width, 1, rows)
-    return (modes, factor)
+    snap, slab = lax.axis_size("snap"), lax.axis_size("slab")
+    total = summed_gram(matrix, snap, slab)
+    modes, factor = factor_and_solve(total, matrix, rows * snap * slab)
+    return (modes.reshape(width, 1, rows), factor)
 
 
 def solution(mesh):

time: 595 us -> 217 us (0.36); the launches traced: 585 us -> 216 us
  waiting for transfers between devices: 229 us -> 35.4 us
  other arithmetic: 203 us -> 10.8 us
  Pallas kernels: 0 us -> 93.2 us
  matrix products: 30.2 us -> 0 us
  local copies, waits for them, and re-layouts: 68.6 us -> 40.9 us
  between operations: 18.4 us -> 0.75 us
    another operation x26 -> x2, other arithmetic: 191 us -> 8.03 us  [the longest x22 124 us: body(): lower = jnp.linalg.cholesky(total / point_count)]
    unnamed x3 -> x0, waiting for transfers between devices: 136 us -> none
    pallas_call x0 -> x2, Pallas kernels: none -> 93.2 us  [the longest x1 48.5 us: summed_gram(): pl.pallas_call(functools.partial(gram_kernel, steps), out_shape=jax.Shape...]
    all_gather x1 -> x0, waiting for transfers between devices: 56.5 us -> none  [reduce_entries(): total = lax.all_gather(share, ('snap', 'slab'), axis=0, tiled=True)]
    another operation x21 -> x0, matrix products: 26.3 us -> none  [the longest x11 16.5 us: body(): jax.scipy.linalg.solve_triangular(lower, matrix.astype(jnp.float32), lowe...]
    another operation x26 -> x0, local copies, waits for them, and re-layouts: 17.1 us -> none
    unnamed x23 -> x9, local copies, waits for them, and re-layouts: 21.5 us -> 14 us
  transfers between devices with their start and end apart: 4 -> 2, of which waited for: 3 -> 1; matrix products, arithmetic and copies ran while one was open for 2% -> 4% of each run, Pallas kernels for 0% -> 0%
where the time goes in v1:
time: 217 us; the launch traced here: 216 us
  Pallas kernels  93.2 us (43%)
  local copies, waits for them, and re-layouts  40.9 us (19%)
  waiting for transfers between devices  35.4 us (16%)
  blocking collectives  27.5 us (13%)
  other arithmetic  10.8 us (5%)
  starting transfers between devices  7.25 us (3%)
    pallas_call x1, Pallas kernels, summed_gram(): pl.pallas_call(functools.partial(gram_kernel, steps), out_shape=jax.Shape...  48.5 us
    pallas_call x1, Pallas kernels, factor_and_solve(): pl.pallas_call(functools.partial(solve_kernel, float(points)), out_shape=...  44.7 us
    ppermute x1, waiting for transfers between devices, with_halo(): lax.ppermute(lax.slice_in_dim(block, block.shape[dim] - width, None, axis...  35.4 us
    all_to_all x1, blocking collectives, body(): lax.all_to_all(flat, 'snap', split_axis=2, concat_axis=0, tiled=True)  27.5 us
    unnamed x9, local copies, waits for them, and re-layouts  14 us
    all_to_all x1, local copies, waits for them, and re-layouts, body(): lax.all_to_all(flat, 'snap', split_axis=2, concat_axis=0, tiled=True)  8.96 us
    another operation x4, local copies, waits for them, and re-layouts, body(): jnp.stack([omega_one, omega_two, omega_three], axis=1).astype(jnp.bfloat16)  8.65 us
    another operation x2, other arithmetic  8.03 us
  transfers between devices with their start and end apart: 2, of which 1 were waited for; matrix products, arithmetic and copies ran while one was open for 4% of the time, Pallas kernels for 0%

profile of v1, /device:TPU:0, one launch (start us, length us, event | category | flops | bytes accessed | tf_op | source)
XLA Modules:
  0.0 215.8 jit_solution(6669280778225599847)
XLA Ops:
  0.6 3.0 %fusion.58 = (bf16[64,2,4,8,128]{4,3,2,1,0:T(8,128)(2,1)S(1)}, bf16[64,2,4,8,128]{4,3,2,1,0:T(8,128)(2,1)}) fusion(bf16[64,3,5,8,128]{4,3,2,1,0:T(8,128)(2,1)} %param.1), kind=kLoop, calls=%fused_computation.101 | loop fusion | bytes 4194304 | tf_op jit(solution)/shard_map/slice | solution.py:24
  3.6 0.0 copy-start
  3.6 6.0 %collective-permute-start = (bf16[64,2,4,8,128]{4,3,2,1,0:T(8,128)(2,1)}, bf16[64,2,4,8,128]{4,3,2,1,0:T(8,128)(2,1)}, u32[]{:S(2)}, u32[]{:S(2)}) collective-permute-start(bf16[64,2,4,8,128]{4,3,2,1,0:T(8,128)(2,1)} %get-tuple-element.12), channel_id=1, source_target_pairs={{0,1},{1,2},{2,3},{3,4},{4,5},{5,6},{6,7},{8,9},{9,10},{10,11},{11... | collective-permute-start | bytes 3145736 | tf_op jit(solution)/shard_map/ppermute | solution.py:21
  9.6 1.1 copy.37
  10.6 1.3 collective-permute-start.1
  11.9 0.0 copy-done
  11.9 0.3 slice_bitcast_fusion.3
  12.2 0.4 pad_convert_fusion
  12.6 0.3 pad_convert_fusion.1
  12.9 3.3 %fusion.45 = bf16[64,5,8,128]{3,2,1,0:T(8,128)(2,1)} fusion(f32[64,5,8,136]{3,2,1,0:T(8,128)S(1)} %pad_convert_fusion, f32[64,5,16,128]{3,2,1,0:T(8,128)S(1)} %pad_convert_fusion.1), kind=kLoop, calls=%fused_computation.73 | loop fusion | flops 7864320 | bytes 21626880 | tf_op jit(solution)/shard_map/convert.14
  16.2 2.2 %stack.12 = bf16[64,1,5120]{2,0,1:T(8,128)(2,1)} reshape(bf16[64,5,8,128]{3,2,1,0:T(8,128)(2,1)} %fusion.45) | data formatting | bytes 1310720 | tf_op jit(solution)/shard_map/stack | solution.py:299
  18.4 35.4 %collective-permute-done = bf16[64,2,4,8,128]{4,3,2,1,0:T(8,128)(2,1)} collective-permute-done((bf16[64,2,4,8,128]{4,3,2,1,0:T(8,128)(2,1)}, bf16[64,2,4,8,128]{4,3,2,1,0:T(8,128)(2,1)}, u32[]{:S(2)}, u32[]{:S(2)}) %collective-permute-start) | collective-permute-done | bytes 1048608 | tf_op jit(solution)/shard_map/ppermute | solution.py:21
  53.8 1.3 copy_dynamic-update-slice_fusion.1
  55.1 0.2 copy_dynamic-update-slice_fusion
  55.3 0.0 collective-permute-done.1
  55.3 1.4 constant_dynamic-update-slice_fusion
  56.7 0.4 fusion.1
  57.1 4.7 %fusion.8 = (bf16[64,5,8,128]{3,2,1,0:T(8,128)(2,1)S(1)}, bf16[64,5,8,128]{3,2,1,0:T(8,128)(2,1)S(1)}) fusion(f32[64,5,8,128]{3,2,1,0:T(8,128)S(1)} %get-tuple-element.10, f32[64,13,8,128]{3,2,1,0:T(8,128)S(1)} %get-tuple-element.6, f32[64,13,8,128]{3,2,1,0:T(8,128)S(1)} %get-tuple-element.7), kind=kLoop, calls=%fused_computation.27 | loop fusion | flops 15728640 | bytes 23592960 | tf_op jit(solution)/shard_map/convert.13
  61.8 0.0 copy-start.1
  61.8 0.3 stack.13
  62.1 1.1 stack.14
  63.2 0.0 copy-done.1
  63.2 1.3 pad_maximum_fusion
  64.6 5.1 %copy.29 = bf16[64,3,5120]{0,1,2:T(4,128)(2,1)} copy(bf16[64,3,5120]{2,0,1:T(8,128)(2,1)S(1)} %pad_maximum_fusion) | data formatting | bytes 3932160 | tf_op jit(solution)/shard_map/stack | solution.py:299
  69.6 5.3 %reshape.36 = bf16[4,2,122880]{2,1,0:T(2,128)(2,1)S(1)} reshape(bf16[5120,3,64]{2,1,0:T(4,128)(2,1)} %bitcast.34) | data formatting | bytes 3932160
  75.0 27.5 %all_to_all.15 = bf16[4,2,122880]{2,1,0:T(2,128)(2,1)} all-to-all(bf16[4,2,122880]{2,1,0:T(2,128)(2,1)S(1)} %reshape.36), channel_id=1, replica_groups=mesh['snap'=4,'slab'=8] {'snap'}, dimensions={0} | all-to-all | bytes 3932160 | tf_op jit(solution)/shard_map/all_to_all | solution.py:302
  102.5 6.1 %reshape.37 = bf16[5120,3,64]{2,1,0:T(4,128)(2,1)} reshape(bf16[4,2,122880]{2,1,0:T(2,128)(2,1)} %all_to_all.15) | data formatting | bytes 3932160
  108.6 9.0 %copy.31 = bf16[4,64,3,1280]{3,2,1,0:T(4,128)(2,1)} copy(bf16[4,64,3,1280]{1,2,3,0:T(4,128)(2,1)} %bitcast.35) | data formatting | bytes 3932160 | tf_op jit(solution)/shard_map/all_to_all | solution.py:302
  117.6 4.9 %reshape.31.m_ref = bf16[768,1280]{1,0:T(8,128)(2,1)S(1)} reshape(bf16[4,64,3,1280]{3,2,1,0:T(4,128)(2,1)} %copy.31) | data formatting | bytes 3932160 | tf_op jit(solution)/shard_map/reshape | solution.py:304
  122.5 48.5 %gram_sum.1.g_ref = f32[2816,128]{1,0:T(8,128)S(1)} custom-call(bf16[768,1280]{1,0:T(8,128)(2,1)S(1)} %reshape.31.m_ref), custom_call_target="tpu_custom_call" | custom-call | tf_op jit(solution)/shard_map/gram_sum/pallas_call | solution.py:138
  171.1 44.7 %factor_solve.1 = (bf16[768,1280]{1,0:T(8,128)(2,1)}, f32[768,768]{1,0:T(8,128)}) custom-call(f32[2816,128]{1,0:T(8,128)S(1)} %gram_sum.1.g_ref, bf16[768,1280]{1,0:T(8,128)(2,1)S(1)} %reshape.31.m_ref), custom_call_target="tpu_custom_call" | custom-call | tf_op jit(solution)/shard_map/factor_solve/pallas_call | solution.py:267
Async XLA Ops:
  3.6 8.3 %copy-start = (bf16[64,3,5,8,128]{4,3,2,1,0:T(8,128)(2,1)S(1)}, bf16[64,3,5,8,128]{4,3,2,1,0:T(8,128)(2,1)}, u32[]{:S(2)}) copy-start(bf16[64,3,5,8,128]{4,3,2,1,0:T(8,128)(2,1)} %param.1) | copy-start | bytes 5898244
  3.6 50.2 %collective-permute-start = (bf16[64,2,4,8,128]{4,3,2,1,0:T(8,128)(2,1)}, bf16[64,2,4,8,128]{4,3,2,1,0:T(8,128)(2,1)}, u32[]{:S(2)}, u32[]{:S(2)}) collective-permute-start(bf16[64,2,4,8,128]{4,3,2,1,0:T(8,128)(2,1)} %get-tuple-element.12), channel_id=1, source_target_pairs={{0,1},{1,2},{2,3},{3,4},{4,5},{5,6},{6,7},{8,9},{9,10},{10,11},{11... | collective-permute-start | bytes 3145736 | tf_op jit(solution)/shard_map/ppermute | solution.py:21
  10.6 44.7 %collective-permute-start.1 = (bf16[64,2,4,8,128]{4,3,2,0,1:T(8,128)(2,1)}, bf16[64,2,4,8,128]{4,3,2,0,1:T(8,128)(2,1)}, u32[]{:S(2)}, u32[]{:S(2)}) collective-permute-start(bf16[64,2,4,8,128]{4,3,2,0,1:T(8,128)(2,1)} %copy.37), channel_id=1, source_target_pairs={{1,0},{2,1},{3,2},{4,3},{5,4},{6,5},{7,6},{9,8},{10,9},{11,10},{12... | collective-permute-start | bytes 3145736 | tf_op jit(solution)/shard_map/ppermute | solution.py:24
  61.8 1.4 copy-start.1

commit v2 on v1

--- a/solution.py
+++ b/solution.py
@@ -61,9 +61,13 @@
     return steps
 
 
-def gram_kernel(steps, m_ref, out_ref, acc_ref, landing, send_sem, recv_sem, gather_send, gather_recv):
-    width = m_ref.shape[0]
+def gram_kernel(
+    sizes, streams, f_ref, m_ref, out_ref, acc_ref, landing,
+    send_sem, recv_sem, gather_send, gather_recv, move_send, move_recv, own_sem,
+):
+    width, columns = m_ref.shape
     blocks = width // BLOCK
+    height = f_ref.shape[0]
     total_rows = acc_ref.shape[0]
     place = {"snap": lax.axis_index("snap"), "slab": lax.axis_index("slab")}
 
@@ -75,9 +79,35 @@
     def device(where):
         return (where["snap"], where["slab"])
 
+    others = [
+        {**place, "snap": lax.rem(place["snap"] + d, sizes["snap"])} for d in range(1, sizes["snap"])
+    ]
+    greeted = others + [partner(axis, bit)[1] for axis, bit in streams[0] if axis == "slab"]
     barrier = pltpu.get_barrier_semaphore()
-    for axis, bit in steps:
-        pl.semaphore_signal(barrier, 1, device_id=device(partner(axis, bit)[1]), device_id_type=MESH)
+    for where in greeted:
+        pl.semaphore_signal(barrier, 1, device_id=device(where), device_id_type=MESH)
+    pl.semaphore_wait(barrier, len(greeted))
+
+    own_rows = pl.ds(pl.multiple_of(place["snap"] * height, 16), height)
+    moves = []
+    for d, where in enumerate(others):
+        strip = pl.ds(pl.multiple_of(where["snap"] * columns, BLOCK), columns)
+        move = pltpu.make_async_remote_copy(
+            src_ref=f_ref.at[:, strip],
+            dst_ref=m_ref.at[own_rows, :],
+            send_sem=move_send.at[d],
+            recv_sem=move_recv.at[d],
+            device_id=device(where),
+            device_id_type=MESH,
+        )
+        move.start()
+        moves.append(move)
+    own_strip = pl.ds(pl.multiple_of(place["snap"] * columns, BLOCK), columns)
+    stay = pltpu.make_async_copy(f_ref.at[:, own_strip], m_ref.at[own_rows, :], own_sem)
+    stay.start()
+    stay.wait()
+    for move in moves:
+        move.wait()
 
     starts, used = upper_offsets(blocks)
     for i in range(blocks):
@@ -90,69 +120,89 @@
         acc_ref[starts[i] : starts[i] + (blocks - i) * BLOCK, :] = tall
     if total_rows > used:
         acc_ref[used:, :] = jnp.zeros((total_rows - used, BLOCK), jnp.float32)
-    pl.semaphore_wait(barrier, len(steps))
-
-    start, length, at = 0, total_rows, 0
+
+    lane_rows = total_rows // len(streams)
+    state = [(t * lane_rows, lane_rows, t * lane_rows) for t in range(len(streams))]
     history = []
-    for index, (axis, bit) in enumerate(steps):
-        half = length // 2
-        is_high, other = partner(axis, bit)
-        keep = pl.multiple_of(start + is_high * half, 8)
-        give = pl.multiple_of(start + (1 - is_high) * half, 8)
-        copy = pltpu.make_async_remote_copy(
-            src_ref=acc_ref.at[pl.ds(give, half)],
-            dst_ref=landing.at[pl.ds(at, half)],
-            send_sem=send_sem.at[index],
-            recv_sem=recv_sem.at[index],
-            device_id=device(other),
-            device_id_type=MESH,
-        )
-        copy.start()
-        copy.wait()
-        acc_ref[pl.ds(keep, half), :] = acc_ref[pl.ds(keep, half), :] + landing[at : at + half, :]
-        history.append((index, axis, bit, keep, half))
-        start, length, at = keep, half, at + half
-    out_ref[pl.ds(start, length), :] = acc_ref[pl.ds(start, length), :]
-    for index, axis, bit, keep, half in reversed(history):
-        other = partner(axis, bit)[1]
-        copy = pltpu.make_async_remote_copy(
-            src_ref=out_ref.at[pl.ds(keep, half)],
-            dst_ref=out_ref.at[pl.ds(keep, half)],
-            send_sem=gather_send.at[index],
-            recv_sem=gather_recv.at[index],
-            device_id=device(other),
-            device_id_type=MESH,
-        )
-        copy.start()
-        copy.wait()
-
-
-def summed_gram(matrix, snap, slab):
-    width, points = matrix.shape
+    for index in range(len(streams[0])):
+        flying = []
+        for t, steps in enumerate(streams):
+            axis, bit = steps[index]
+            start, length, at = state[t]
+            half = length // 2
+            is_high, other = partner(axis, bit)
+            keep = pl.multiple_of(start + is_high * half, 8)
+            give = pl.multiple_of(start + (1 - is_high) * half, 8)
+            copy = pltpu.make_async_remote_copy(
+                src_ref=acc_ref.at[pl.ds(give, half)],
+                dst_ref=landing.at[pl.ds(at, half)],
+                send_sem=send_sem.at[t, index],
+                recv_sem=recv_sem.at[t, index],
+                device_id=device(other),
+                device_id_type=MESH,
+            )
+            copy.start()
+            flying.append((copy, keep, half, at))
+            state[t] = (keep, half, at + half)
+        for copy, keep, half, at in flying:
+            copy.wait()
+            acc_ref[pl.ds(keep, half), :] = acc_ref[pl.ds(keep, half), :] + landing[at : at + half, :]
+        history.append([(keep, half) for _, keep, half, _ in flying])
+    for start, length, _ in state:
+        out_ref[pl.ds(start, length), :] = acc_ref[pl.ds(start, length), :]
+    for index in reversed(range(len(streams[0]))):
+        flying = []
+        for t, steps in enumerate(streams):
+            axis, bit = steps[index]
+            keep, half = history[index][t]
+            copy = pltpu.make_async_remote_copy(
+                src_ref=out_ref.at[pl.ds(keep, half)],
+                dst_ref=out_ref.at[pl.ds(keep, half)],
+                send_sem=gather_send.at[t, index],
+                recv_sem=gather_recv.at[t, index],
+                device_id=device(partner(axis, bit)[1]),
+                device_id_type=MESH,
+            )
+            copy.start()
+            flying.append(copy)
+        for copy in flying:
+            copy.wait()
+
+
+def summed_gram(flat, snap, slab):
+    height, points = flat.shape
+    width, columns = height * snap, points // snap
     used = upper_offsets(width // BLOCK)[1]
     devices = snap * slab
-    share = -(-used // (devices * 8)) * 8
-    rows = share * devices
     steps = halving_steps(snap, slab)
-    count = max(len(steps), 1)
+    lead, rest = steps[:1], steps[1:]
+    shifts = (0, len(halving_steps(snap, 1)) - 1, len(halving_steps(snap, 1)))
+    streams = [lead + rest[shift:] + rest[:shift] for shift in shifts]
+    share = -(-used // (len(streams) * devices * 8)) * 8
+    rows = share * devices * len(streams)
+    vmem = pl.BlockSpec(memory_space=pltpu.VMEM)
+    stages = pltpu.SemaphoreType.DMA((len(streams), len(steps)))
+    moves = pltpu.SemaphoreType.DMA((snap,))
     return pl.pallas_call(
-        functools.partial(gram_kernel, steps),
-        out_shape=jax.ShapeDtypeStruct((rows, BLOCK), jnp.float32),
-        in_specs=[pl.BlockSpec(memory_space=pltpu.VMEM)],
-        out_specs=pl.BlockSpec(memory_space=pltpu.VMEM),
+        functools.partial(gram_kernel, {"snap": snap, "slab": slab}, streams),
+        out_shape=(
+            jax.ShapeDtypeStruct((width, columns), flat.dtype),
+            jax.ShapeDtypeStruct((rows, BLOCK), jnp.float32),
+        ),
+        in_specs=[vmem],
+        out_specs=(vmem, vmem),
         scratch_shapes=[
             pltpu.VMEM((rows, BLOCK), jnp.float32),
             pltpu.VMEM((rows, BLOCK), jnp.float32),
-            pltpu.SemaphoreType.DMA((count,)),
-            pltpu.SemaphoreType.DMA((count,)),
-            pltpu.SemaphoreType.DMA((count,)),
-            pltpu.SemaphoreType.DMA((count,)),
+            stages, stages, stages, stages,
+            moves, moves,
+            pltpu.SemaphoreType.DMA,
         ],
         compiler_params=pltpu.CompilerParams(
             collective_id=1, has_side_effects=True, vmem_limit_bytes=VMEM_LIMIT
         ),
         name="gram_sum",
-    )(matrix)
+    )(flat)
 
 
 def factor_diagonal(d_ref, w_ref, out_ref, spread):
@@ -297,14 +347,10 @@
     omega_two = derive(first, 3) - differ(third_rim, 1, planes)
     omega_three = differ(second_rim, 1, planes) - derive(first, 2)
     vorticity = jnp.stack([omega_one, omega_two, omega_three], axis=1).astype(jnp.bfloat16)
-    local_snaps = vorticity.shape[0]
-    flat = vorticity.reshape(local_snaps, 3, -1)
-    regrouped = lax.all_to_all(flat, "snap", split_axis=2, concat_axis=0, tiled=True)
-    width = regrouped.shape[0] * 3
-    matrix = regrouped.reshape(width, -1)
-    rows = matrix.shape[1]
+    flat = vorticity.reshape(vorticity.shape[0] * 3, -1)
     snap, slab = lax.axis_size("snap"), lax.axis_size("slab")
-    total = summed_gram(matrix, snap, slab)
+    matrix, total = summed_gram(flat, snap, slab)
+    width, rows = matrix.shape
     modes, factor = factor_and_solve(total, matrix, rows * snap * slab)
     return (modes.reshape(width, 1, rows), factor)
 

time: 217 us -> 174 us (0.80)
  local copies, waits for them, and re-layouts: 40.9 us -> 6.87 us
  blocking collectives: 27.5 us -> 0 us
  Pallas kernels: 93.2 us -> 111 us
  waiting for transfers between devices: 35.4 us -> 39.8 us
    all_to_all x1 -> x0, blocking collectives: 27.5 us -> none  [body(): lax.all_to_all(flat, 'snap', split_axis=2, concat_axis=0, tiled=True)]
    pallas_call x1, Pallas kernels: 48.5 us -> 66.1 us  [summed_gram(): pl.pallas_call(functools.partial(gram_kernel, {'snap': snap, 'slab': slab...]
    unnamed x9 -> x5, local copies, waits for them, and re-layouts: 14 us -> 0.37 us
    all_to_all x1 -> x0, local copies, waits for them, and re-layouts: 8.96 us -> none  [body(): lax.all_to_all(flat, 'snap', split_axis=2, concat_axis=0, tiled=True)]
    another operation x2 -> x0, other arithmetic: 8.03 us -> none
    another operation x4 -> x1, local copies, waits for them, and re-layouts: 8.65 us -> 1.61 us  [body(): jnp.stack([omega_one, omega_two, omega_three], axis=1).astype(jnp.bfloat16)]
    another operation x1 -> x3, other arithmetic: 1.3 us -> 7.5 us  [body(): jnp.stack([omega_one, omega_two, omega_three], axis=1).astype(jnp.bfloat16)]
    reshape x1 -> x0, local copies, waits for them, and re-layouts: 4.9 us -> none  [body(): matrix = regrouped.reshape(width, -1)]
  transfers between devices with their start and end apart: 2 -> 2, of which waited for: 1 -> 1; matrix products, arithmetic and copies ran while one was open for 4% -> 2% of each run, Pallas kernels for 0% -> 0%
where the time goes in v2:
time: 174 us
  Pallas kernels  111 us (64%)
  waiting for transfers between devices  39.8 us (23%)
  other arithmetic  8.93 us (5%)
  local copies, waits for them, and re-layouts  6.87 us (4%)
  starting transfers between devices  6.36 us (4%)
    pallas_call x1, Pallas kernels, summed_gram(): pl.pallas_call(functools.partial(gram_kernel, {'snap': snap, 'slab': slab...  66.1 us
    pallas_call x1, Pallas kernels, factor_and_solve(): pl.pallas_call(functools.partial(solve_kernel, float(points)), out_shape=...  44.7 us
    ppermute x1, waiting for transfers between devices, with_halo(): lax.ppermute(lax.slice_in_dim(block, block.shape[dim] - width, None, axis...  39.8 us
    another operation x3, other arithmetic, body(): jnp.stack([omega_one, omega_two, omega_three], axis=1).astype(jnp.bfloat16)  7.5 us
    ppermute x1, starting transfers between devices, with_halo(): lax.ppermute(lax.slice_in_dim(block, block.shape[dim] - width, None, axis...  5.07 us
  transfers between devices with their start and end apart: 2, of which 1 were waited for; matrix products, arithmetic and copies ran while one was open for 2% of the time, Pallas kernels for 0%

profile of v2, /device:TPU:0, one launch (start us, length us, event | category | flops | bytes accessed | tf_op | source)
XLA Modules:
  0.0 173.6 jit_solution(11636684847136651319)
XLA Ops:
  0.6 2.0 %fusion.61 = (bf16[64,2,4,8,128]{4,3,2,1,0:T(8,128)(2,1)S(1)}, bf16[64,2,4,8,128]{4,3,2,1,0:T(8,128)(2,1)S(1)}) fusion(bf16[64,3,5,8,128]{4,3,2,1,0:T(8,128)(2,1)} %param.1), kind=kLoop, calls=%fused_computation.104 | loop fusion | bytes 4194304 | tf_op jit(solution)/shard_map/slice | solution.py:24
  2.6 0.0 copy-start
  2.6 5.1 %collective-permute-start = (bf16[64,2,4,8,128]{4,3,2,1,0:T(8,128)(2,1)S(1)}, bf16[64,2,4,8,128]{4,3,2,1,0:T(8,128)(2,1)S(1)}, u32[]{:S(2)}, u32[]{:S(2)}) collective-permute-start(bf16[64,2,4,8,128]{4,3,2,1,0:T(8,128)(2,1)S(1)} %get-tuple-element.16), channel_id=1, source_target_pairs={{0,1},{1,2},{2,3},{3,4},{4,5},{5,6},{6,7},{8,9},{9,10},{10,11},{11... | collective-permute-start | bytes 3145736 | tf_op jit(solution)/shard_map/ppermute | solution.py:21
  7.7 0.1 copy.12
  7.8 1.3 collective-permute-start.1
  9.1 0.0 copy-done
  9.1 0.3 slice_bitcast_fusion.3
  9.4 0.4 pad_convert_fusion
  9.8 0.3 pad_convert_fusion.1
  10.1 2.6 %fusion.58 = bf16[64,1,5,8,128]{4,3,2,0,1:T(8,128)(2,1)S(1)} fusion(f32[64,5,8,136]{3,2,1,0:T(8,128)S(1)} %pad_convert_fusion, f32[64,5,16,128]{3,2,1,0:T(8,128)S(1)} %pad_convert_fusion.1), kind=kLoop, calls=%fused_computation.100 | loop fusion | flops 7864320 | bytes 21626880 | tf_op jit(solution)/shard_map/stack | solution.py:349
  12.7 39.8 %collective-permute-done = bf16[64,2,4,8,128]{4,3,2,1,0:T(8,128)(2,1)S(1)} collective-permute-done((bf16[64,2,4,8,128]{4,3,2,1,0:T(8,128)(2,1)S(1)}, bf16[64,2,4,8,128]{4,3,2,1,0:T(8,128)(2,1)S(1)}, u32[]{:S(2)}, u32[]{:S(2)}) %collective-permute-start) | collective-permute-done | bytes 1048608 | tf_op jit(solution)/shard_map/ppermute | solution.py:21
  52.5 0.1 copy_dynamic-update-slice_fusion.1
  52.6 0.2 copy_dynamic-update-slice_fusion
  52.8 0.0 collective-permute-done.1
  52.8 0.1 constant_dynamic-update-slice_fusion
  53.0 0.4 fusion.1
  53.4 4.7 %fusion.60 = (bf16[64,1,5,8,128]{4,3,2,0,1:T(8,128)(2,1)S(1)}, bf16[64,1,5,8,128]{4,3,2,0,1:T(8,128)(2,1)S(1)}) fusion(f32[64,13,8,128]{3,2,1,0:T(8,128)S(1)} %get-tuple-element.10, f32[64,5,8,128]{3,2,1,0:T(8,128)S(1)} %get-tuple-element.14, f32[64,13,8,128]{3,2,1,0:T(8,128)S(1)} %get-tuple-element.11), kind=kLoop, calls=%fused_computation.102 | loop fusion | flops 15728640 | bytes 23592960 | tf_op jit(solution)/shard_map/stack | solution.py:349
  58.1 0.2 pad_maximum_fusion
  58.3 1.6 copy.8
  59.9 2.8 %convert_element_type.45.f_ref = bf16[192,5120]{1,0:T(8,128)(2,1)S(1)} reshape(bf16[64,3,5,8,128]{4,3,2,1,0:T(8,128)(2,1)} %copy.8) | data formatting | bytes 3932160 | tf_op jit(solution)/shard_map/convert_element_type | solution.py:349
  62.7 66.1 %gram_sum.1 = (bf16[768,1280]{1,0:T(8,128)(2,1)S(1)}, f32[3072,128]{1,0:T(8,128)S(1)}) custom-call(bf16[192,5120]{1,0:T(8,128)(2,1)S(1)} %convert_element_type.45.f_ref), custom_call_target="tpu_custom_call" | custom-call | tf_op jit(solution)/shard_map/gram_sum/pallas_call | solution.py:186
  128.9 44.7 %factor_solve.1 = (bf16[768,1280]{1,0:T(8,128)(2,1)}, f32[768,768]{1,0:T(8,128)}) custom-call(f32[3072,128]{1,0:T(8,128)S(1)} %get-tuple-element.6.g_ref, bf16[768,1280]{1,0:T(8,128)(2,1)S(1)} %get-tuple-element.7.m_ref), custom_call_target="tpu_custom_call" | custom-call | tf_op jit(solution)/shard_map/factor_solve/pallas_call | solution.py:317
Async XLA Ops:
  2.6 6.5 %copy-start = (bf16[64,3,5,8,128]{4,3,2,1,0:T(8,128)(2,1)S(1)}, bf16[64,3,5,8,128]{4,3,2,1,0:T(8,128)(2,1)}, u32[]{:S(2)}) copy-start(bf16[64,3,5,8,128]{4,3,2,1,0:T(8,128)(2,1)} %param.1) | copy-start | bytes 5898244
  2.6 49.9 %collective-permute-start = (bf16[64,2,4,8,128]{4,3,2,1,0:T(8,128)(2,1)S(1)}, bf16[64,2,4,8,128]{4,3,2,1,0:T(8,128)(2,1)S(1)}, u32[]{:S(2)}, u32[]{:S(2)}) collective-permute-start(bf16[64,2,4,8,128]{4,3,2,1,0:T(8,128)(2,1)S(1)} %get-tuple-element.16), channel_id=1, source_target_pairs={{0,1},{1,2},{2,3},{3,4},{4,5},{5,6},{6,7},{8,9},{9,10},{10,11},{11... | collective-permute-start | bytes 3145736 | tf_op jit(solution)/shard_map/ppermute | solution.py:21
  7.8 45.0 %collective-permute-start.1 = (bf16[64,2,4,8,128]{4,3,2,0,1:T(8,128)(2,1)S(1)}, bf16[64,2,4,8,128]{4,3,2,0,1:T(8,128)(2,1)S(1)}, u32[]{:S(2)}, u32[]{:S(2)}) collective-permute-start(bf16[64,2,4,8,128]{4,3,2,0,1:T(8,128)(2,1)S(1)} %copy.12), channel_id=1, source_target_pairs={{1,0},{2,1},{3,2},{4,3},{5,4},{6,5},{7,6},{9,8},{10,9},{11,10},{12... | collective-permute-start | bytes 3145736 | tf_op jit(solution)/shard_map/ppermute | solution.py:24

commit v3 on v2

--- a/solution.py
+++ b/solution.py
@@ -250,7 +250,7 @@
             w_ref[t * group : (t + 1) * group, :] = aside
 
 
-def solve_kernel(points, g_ref, m_ref, modes_ref, factor_ref, work, inverse, diag, side, dinv, spread):
+def solve_kernel(points, g_ref, m_ref, modes_ref, factor_ref, work, diag, side, dinv, spread):
     width = m_ref.shape[0]
     blocks = width // BLOCK
     starts, _ = upper_offsets(blocks)
@@ -261,20 +261,24 @@
     for i in range(blocks):
         for j in range(blocks):
             here = (slice(i * BLOCK, (i + 1) * BLOCK), slice(j * BLOCK, (j + 1) * BLOCK))
-            there = (here[0], slice(width + j * BLOCK, width + (j + 1) * BLOCK))
             if j >= i:
                 row = starts[i] + (j - i) * BLOCK
                 block = g_ref[row : row + BLOCK, :] / points
                 work[here] = block if i == j else block.T
             else:
                 work[here] = zero
-            work[there] = eye if i == j else zero
 
     def step(k, carry):
         base = pl.multiple_of(k * BLOCK, BLOCK)
         diag[...] = work[pl.ds(base, BLOCK), pl.ds(base, BLOCK)]
         side[...] = eye
         factor_diagonal(diag, side, dinv, spread)
+        corner = jnp.dot(
+            dinv[...], work[pl.ds(base, BLOCK), pl.ds(base, BLOCK)],
+            precision=HI, preferred_element_type=jnp.float32,
+        )
+        factor_ref[pl.ds(base, BLOCK), pl.ds(base, BLOCK)] = jnp.where(lane >= rank, corner, 0.0)
+        work[pl.ds(base, BLOCK), pl.ds(base, BLOCK)] = eye
         panel = jnp.dot(
             dinv[...], work[pl.ds(base, BLOCK), :], precision=HI, preferred_element_type=jnp.float32
         )
@@ -283,6 +287,7 @@
         def update(i, inner):
             low = pl.multiple_of(i * BLOCK, BLOCK)
             left = work[pl.ds(base, BLOCK), pl.ds(low, BLOCK)].T
+            work[pl.ds(low, BLOCK), pl.ds(base, BLOCK)] = zero
             work[pl.ds(low, BLOCK), :] -= jnp.dot(
                 left, work[pl.ds(base, BLOCK), :], precision=HI, preferred_element_type=jnp.float32
             )
@@ -298,12 +303,10 @@
             cols = slice(j * BLOCK, (j + 1) * BLOCK)
             if j < i:
                 factor_ref[rows, cols] = zero
-            elif j == i:
-                factor_ref[rows, cols] = jnp.where(lane >= rank, work[rows, cols], 0.0)
-            else:
+            elif j > i:
                 factor_ref[rows, cols] = work[rows, cols]
         depth = (i + 1) * BLOCK
-        part = work[rows, width : width + depth]
+        part = work[rows, :depth]
         top = part.astype(jnp.bfloat16)
         rest = (part - top.astype(jnp.float32)).astype(jnp.bfloat16)
         solved = jnp.dot(top, m_ref[:depth, :], preferred_element_type=jnp.float32)
@@ -323,8 +326,7 @@
         in_specs=[vmem, vmem],
         out_specs=(vmem, vmem),
         scratch_shapes=[
-            pltpu.VMEM((width, 2 * width), jnp.float32),
-            pltpu.VMEM((8, BLOCK), jnp.float32),
+            pltpu.VMEM((width, width), jnp.float32),
             pltpu.VMEM((BLOCK, BLOCK), jnp.float32),
             pltpu.VMEM((BLOCK, BLOCK), jnp.float32),
             pltpu.VMEM((BLOCK, BLOCK), jnp.float32),

time: 174 us -> 168 us (0.966)
  Pallas kernels: 111 us -> 105 us
    pallas_call x1, Pallas kernels: 44.7 us -> 39.1 us  [factor_and_solve(): pl.pallas_call(functools.partial(solve_kernel, float(points)), out_shape=...]
where the time goes in v3:
time: 168 us
  Pallas kernels  105 us (62%)
  waiting for transfers between devices  39.8 us (24%)
  other arithmetic  8.93 us (5%)
  local copies, waits for them, and re-layouts  6.87 us (4%)
  starting transfers between devices  6.36 us (4%)
    pallas_call x1, Pallas kernels, summed_gram(): pl.pallas_call(functools.partial(gram_kernel, {'snap': snap, 'slab': slab...  66.1 us
    ppermute x1, waiting for transfers between devices, with_halo(): lax.ppermute(lax.slice_in_dim(block, block.shape[dim] - width, None, axis...  39.8 us
    pallas_call x1, Pallas kernels, factor_and_solve(): pl.pallas_call(functools.partial(solve_kernel, float(points)), out_shape=...  39.1 us
    another operation x3, other arithmetic, body(): jnp.stack([omega_one, omega_two, omega_three], axis=1).astype(jnp.bfloat16)  7.5 us
    ppermute x1, starting transfers between devices, with_halo(): lax.ppermute(lax.slice_in_dim(block, block.shape[dim] - width, None, axis...  5.07 us
  transfers between devices with their start and end apart: 2, of which 1 were waited for; matrix products, arithmetic and copies ran while one was open for 2% of the time, Pallas kernels for 0%

profile of v3, /device:TPU:0, one launch (start us, length us, event | category | flops | bytes accessed | tf_op | source)
XLA Modules:
  0.0 167.9 jit_solution(11663849200575210974)
XLA Ops:
  0.6 2.0 %fusion.61 = (bf16[64,2,4,8,128]{4,3,2,1,0:T(8,128)(2,1)S(1)}, bf16[64,2,4,8,128]{4,3,2,1,0:T(8,128)(2,1)S(1)}) fusion(bf16[64,3,5,8,128]{4,3,2,1,0:T(8,128)(2,1)} %param.1), kind=kLoop, calls=%fused_computation.104 | loop fusion | bytes 4194304 | tf_op jit(solution)/shard_map/slice | solution.py:24
  2.6 0.0 copy-start
  2.6 5.1 %collective-permute-start = (bf16[64,2,4,8,128]{4,3,2,1,0:T(8,128)(2,1)S(1)}, bf16[64,2,4,8,128]{4,3,2,1,0:T(8,128)(2,1)S(1)}, u32[]{:S(2)}, u32[]{:S(2)}) collective-permute-start(bf16[64,2,4,8,128]{4,3,2,1,0:T(8,128)(2,1)S(1)} %get-tuple-element.16), channel_id=1, source_target_pairs={{0,1},{1,2},{2,3},{3,4},{4,5},{5,6},{6,7},{8,9},{9,10},{10,11},{11... | collective-permute-start | bytes 3145736 | tf_op jit(solution)/shard_map/ppermute | solution.py:21
  7.7 0.1 copy.12
  7.8 1.3 collective-permute-start.1
  9.1 0.0 copy-done
  9.1 0.3 slice_bitcast_fusion.3
  9.4 0.4 pad_convert_fusion
  9.8 0.3 pad_convert_fusion.1
  10.1 2.6 %fusion.58 = bf16[64,1,5,8,128]{4,3,2,0,1:T(8,128)(2,1)S(1)} fusion(f32[64,5,8,136]{3,2,1,0:T(8,128)S(1)} %pad_convert_fusion, f32[64,5,16,128]{3,2,1,0:T(8,128)S(1)} %pad_convert_fusion.1), kind=kLoop, calls=%fused_computation.100 | loop fusion | flops 7864320 | bytes 21626880 | tf_op jit(solution)/shard_map/stack | solution.py:351
  12.7 39.8 %collective-permute-done = bf16[64,2,4,8,128]{4,3,2,1,0:T(8,128)(2,1)S(1)} collective-permute-done((bf16[64,2,4,8,128]{4,3,2,1,0:T(8,128)(2,1)S(1)}, bf16[64,2,4,8,128]{4,3,2,1,0:T(8,128)(2,1)S(1)}, u32[]{:S(2)}, u32[]{:S(2)}) %collective-permute-start) | collective-permute-done | bytes 1048608 | tf_op jit(solution)/shard_map/ppermute | solution.py:21
  52.5 0.1 copy_dynamic-update-slice_fusion.1
  52.6 0.2 copy_dynamic-update-slice_fusion
  52.8 0.0 collective-permute-done.1
  52.8 0.1 constant_dynamic-update-slice_fusion
  53.0 0.4 fusion.1
  53.4 4.7 %fusion.60 = (bf16[64,1,5,8,128]{4,3,2,0,1:T(8,128)(2,1)S(1)}, bf16[64,1,5,8,128]{4,3,2,0,1:T(8,128)(2,1)S(1)}) fusion(f32[64,13,8,128]{3,2,1,0:T(8,128)S(1)} %get-tuple-element.10, f32[64,5,8,128]{3,2,1,0:T(8,128)S(1)} %get-tuple-element.14, f32[64,13,8,128]{3,2,1,0:T(8,128)S(1)} %get-tuple-element.11), kind=kLoop, calls=%fused_computation.102 | loop fusion | flops 15728640 | bytes 23592960 | tf_op jit(solution)/shard_map/stack | solution.py:351
  58.1 0.2 pad_maximum_fusion
  58.3 1.6 copy.8
  59.9 2.8 %convert_element_type.45.f_ref = bf16[192,5120]{1,0:T(8,128)(2,1)S(1)} reshape(bf16[64,3,5,8,128]{4,3,2,1,0:T(8,128)(2,1)} %copy.8) | data formatting | bytes 3932160 | tf_op jit(solution)/shard_map/convert_element_type | solution.py:351
  62.7 66.1 %gram_sum.1 = (bf16[768,1280]{1,0:T(8,128)(2,1)S(1)}, f32[3072,128]{1,0:T(8,128)S(1)}) custom-call(bf16[192,5120]{1,0:T(8,128)(2,1)S(1)} %convert_element_type.45.f_ref), custom_call_target="tpu_custom_call" | custom-call | tf_op jit(solution)/shard_map/gram_sum/pallas_call | solution.py:186
  128.9 39.1 %factor_solve.1 = (bf16[768,1280]{1,0:T(8,128)(2,1)}, f32[768,768]{1,0:T(8,128)}) custom-call(f32[3072,128]{1,0:T(8,128)S(1)} %get-tuple-element.6.g_ref, bf16[768,1280]{1,0:T(8,128)(2,1)S(1)} %get-tuple-element.7.m_ref), custom_call_target="tpu_custom_call" | custom-call | tf_op jit(solution)/shard_map/factor_solve/pallas_call | solution.py:320
Async XLA Ops:
  2.6 6.5 %copy-start = (bf16[64,3,5,8,128]{4,3,2,1,0:T(8,128)(2,1)S(1)}, bf16[64,3,5,8,128]{4,3,2,1,0:T(8,128)(2,1)}, u32[]{:S(2)}) copy-start(bf16[64,3,5,8,128]{4,3,2,1,0:T(8,128)(2,1)} %param.1) | copy-start | bytes 5898244
  2.6 49.9 %collective-permute-start = (bf16[64,2,4,8,128]{4,3,2,1,0:T(8,128)(2,1)S(1)}, bf16[64,2,4,8,128]{4,3,2,1,0:T(8,128)(2,1)S(1)}, u32[]{:S(2)}, u32[]{:S(2)}) collective-permute-start(bf16[64,2,4,8,128]{4,3,2,1,0:T(8,128)(2,1)S(1)} %get-tuple-element.16), channel_id=1, source_target_pairs={{0,1},{1,2},{2,3},{3,4},{4,5},{5,6},{6,7},{8,9},{9,10},{10,11},{11... | collective-permute-start | bytes 3145736 | tf_op jit(solution)/shard_map/ppermute | solution.py:21
  7.8 45.0 %collective-permute-start.1 = (bf16[64,2,4,8,128]{4,3,2,0,1:T(8,128)(2,1)S(1)}, bf16[64,2,4,8,128]{4,3,2,0,1:T(8,128)(2,1)S(1)}, u32[]{:S(2)}, u32[]{:S(2)}) collective-permute-start(bf16[64,2,4,8,128]{4,3,2,0,1:T(8,128)(2,1)S(1)} %copy.12), channel_id=1, source_target_pairs={{1,0},{2,1},{3,2},{4,3},{5,4},{6,5},{7,6},{9,8},{10,9},{11,10},{12... | collective-permute-start | bytes 3145736 | tf_op jit(solution)/shard_map/ppermute | solution.py:24
